TPU v7x, 512 devices: a whole 4x4x16 slice. The times are simulated.
512 devices in a mesh: dp: 4 (over y), ctx: 64 (over x, z), mp: 2 (over core).
Axes of the slice: x: 4, y: 4, z: 16, core: 2. Of those that a mesh axis runs over, the one named last changes fastest.
Arguments:
- features: bfloat16 [4, 8192, 3, 4096], P('dp', 'ctx', None, 'mp'), may hold values from -6 to 6
- conv_weight: float32 [7, 3, 4096], P(None, None, 'mp'), may hold values from -2 to 2
- log_rate: float32 [8, 32], P(None, 'mp'), as said below
- residues: float32 [8, 4096], P(None, 'mp'), may hold values from -4 to 4
- skip_weight: float32 [4096], P('mp'), may hold values from 0.5 to 1.5
- norm_gain: float32 [4096], P('mp'), may hold values from 0.5 to 1.5
- cotangent: bfloat16 [4, 8192, 4096], P('dp', 'ctx', 'mp'), may hold values from -6 to 6
Outputs:
- block_out: bfloat16 [4, 8192, 4096], P('dp', 'ctx', 'mp')
- feature_grad: bfloat16 [4, 8192, 3, 4096], P('dp', 'ctx', None, 'mp')
- conv_grad: float32 [7, 3, 4096], P(None, None, 'mp')
- rate_grad: float32 [8, 32], P(None, 'mp')
- residue_grad: float32 [8, 4096], P(None, 'mp')
- skip_grad: float32 [4096], P('mp')
- gain_grad: float32 [4096], P('mp')
Inputs may be any that keep to these rules, and one draw needn't show every extreme that they name: log_rate lies between ln(1 / 1048576) and ln(1 / 16).
All inputs are finite; a program needn't handle non-finite values.
Results may differ from a plain program's by a relative error of at most 0.0011.
Values may be sent and summed in bfloat16 or wider, within the bound.
No kernel may reach another device: no remote copies, remote signals or barrier semaphores. Data moves between devices by JAX's collectives and lax.ppermute only.
A program may use at most 128 MiB of HBM per device.

v0:
```python
import jax
import jax.numpy as jnp
from jax import lax
from jax.sharding import PartitionSpec as P

D = 4096
EPSILON = 1e-06
HIGHEST = lax.Precision.HIGHEST


def passed_along(value, axis, steps):
    count = lax.axis_size(axis)
    leading, last = (max(0, -steps), min(count, count - steps))
    return lax.ppermute(value, axis, [(source, source + steps) for source in range(leading, last)])


def carried_in(part, axis, combine, identity, reverse):
    count = lax.axis_size(axis)
    place = lax.axis_index(axis)
    ahead = count - 1 - place if reverse else place
    gathered = jax.tree.map(lambda a: lax.all_gather(a, axis), part)
    state = jax.tree.map(lambda a, e: jnp.zeros_like(a) + jnp.asarray(e, a.dtype), part, identity)

    def one(lap, state):
        source = count - 1 - lap if reverse else lap
        return combine(
            state, jax.tree.map(lambda a: lax.dynamic_index_in_dim(a, source, 0, False), gathered)
        )

    return lax.fori_loop(0, ahead, one, state)


def decay_matrix(rate_row, length):
    places = jnp.arange(length, dtype=jnp.float32)
    lagged = places[:, None] - places[None, :]
    clipped = jnp.maximum(lagged, 0.0)
    matrix = jnp.where(lagged >= 0, jnp.exp(-rate_row[:, None, None] * clipped), 0.0)
    return (matrix, clipped)


def compose_back(earlier, later):
    return (earlier[0] * later[0], earlier[1] * later[0][..., None] + later[1])


def local(features, conv_weight, log_rate, residues, skip_weight, norm_gain, cotangent):
    local_feats = features[0]
    length = local_feats.shape[0]
    channels = local_feats.shape[2]
    pole_count = log_rate.shape[0]
    groups_here = log_rate.shape[1]
    group_size = channels // groups_here
    halo_rows = conv_weight.shape[0] - 1
    previous = passed_along(local_feats[length - halo_rows :], "ctx", 1)
    extended = jnp.concatenate([previous, local_feats], axis=0)
    filtered = conv_weight[0] * extended[halo_rows : halo_rows + length]
    for offset in range(1, halo_rows + 1):
        filtered = (
            filtered
            + conv_weight[offset] * extended[halo_rows - offset : halo_rows - offset + length]
        )
    query_rows = filtered[:, 0]
    key_rows = filtered[:, 1]
    value_rows = filtered[:, 2]
    product = key_rows * value_rows
    rate_rows = jnp.exp(log_rate).T
    grouped = product.reshape(length, groups_here, group_size).transpose(1, 0, 2)
    places = jnp.arange(length, dtype=jnp.float32)
    tail_lag = length - 1.0 - places
    block_decay = jnp.exp(-rate_rows * length)

    def forward_plain(pieces):
        rate_row, product_block = pieces
        matrix, clipped = decay_matrix(rate_row, length)
        return jnp.einsum("pts,sc->ptc", matrix, product_block, precision=HIGHEST)

    local_states = lax.map(forward_plain, (rate_rows, grouped))
    end_rows = local_states[:, :, length - 1, :]
    carried = carried_in(
        (block_decay, end_rows),
        "ctx",
        compose_back,
        (jnp.ones_like(block_decay), jnp.zeros_like(end_rows)),
        False,
    )
    state_in = carried[1]
    head_decay = jnp.exp(-rate_rows[:, :, None] * (places + 1.0))
    states = local_states + head_decay[..., None] * state_in[:, :, None, :]
    weights = residues.reshape(pole_count, groups_here, group_size).transpose(1, 0, 2)
    modal_part = jnp.einsum("gptc,gpc->tgc", states, weights, precision=HIGHEST).reshape(
        length, channels
    )
    branch = modal_part + skip_weight * product
    gated_rows = query_rows * branch
    seed_grad = cotangent[0].astype(jnp.float32)
    scaled_grad = norm_gain * seed_grad
    square_sum = lax.psum(jnp.sum(gated_rows * gated_rows, axis=1), "mp")
    inv_rms = lax.rsqrt(square_sum / D + EPSILON)[:, None]
    normed = gated_rows * inv_rms
    block_out = (norm_gain * normed).astype(jnp.bfloat16)
    slope_sum = lax.psum(jnp.sum(scaled_grad * gated_rows, axis=1), "mp")
    gain_local = jnp.sum(seed_grad * normed, axis=0)
    dgated = scaled_grad * inv_rms - gated_rows * (
        slope_sum[:, None] * inv_rms * inv_rms * inv_rms / D
    )
    dquery = dgated * branch
    dbranch = dgated * query_rows
    skip_local = jnp.sum(dbranch * product, axis=0)
    dgrouped = dbranch.reshape(length, groups_here, group_size).transpose(1, 0, 2)
    back_in = jnp.einsum("gpt,gtc->gpc", head_decay, dgrouped, precision=HIGHEST)
    returned = carried_in(
        (block_decay, back_in),
        "ctx",
        compose_back,
        (jnp.ones_like(block_decay), jnp.zeros_like(back_in)),
        True,
    )
    later_in = returned[1]

    def backward_adjoint(pieces):
        (
            rate_row,
            product_block,
            grad_block,
            state_block,
            weight_row,
            later_row,
            start_row,
            slope_row,
        ) = pieces
        matrix, clipped = decay_matrix(rate_row, length)
        residue_part = jnp.sum(grad_block[None] * state_block, axis=1)
        tail_row = jnp.exp(-rate_row[:, None] * tail_lag)
        adjoint = (
            jnp.einsum("pts,tc->psc", matrix, grad_block, precision=HIGHEST)
            + tail_row[..., None] * later_row[:, None, :]
        )
        inner = (
            jnp.sum(adjoint[:, 1:, :] * state_block[:, : length - 1, :], axis=1)
            + adjoint[:, 0, :] * start_row
        )
        rate_part = -jnp.exp(-rate_row) * jnp.sum(weight_row * inner, axis=1)
        return (residue_part, rate_part, jnp.sum(weight_row[:, None, :] * adjoint, axis=0))

    residue_parts, rate_parts, dproduct_groups = lax.map(
        backward_adjoint,
        (rate_rows, grouped, dgrouped, states, weights, later_in, state_in, state_in),
    )
    residue_local = residue_parts.transpose(1, 0, 2).reshape(pole_count, channels)
    rate_local = rate_parts.T * jnp.exp(log_rate)
    dproduct = dproduct_groups.transpose(1, 0, 2).reshape(length, channels) + dbranch * skip_weight
    dfiltered = jnp.stack([dquery, dproduct * value_rows, dproduct * key_rows], axis=1)
    zeros_rim = jnp.zeros((halo_rows, 3, channels), jnp.float32)
    padded_grad = jnp.concatenate([zeros_rim, dfiltered, zeros_rim], axis=0)
    dextended = conv_weight[0] * padded_grad[0 : length + halo_rows]
    for offset in range(1, halo_rows + 1):
        dextended = (
            dextended + conv_weight[offset] * padded_grad[offset : offset + length + halo_rows]
        )
    conv_local = jnp.stack(
        [
            jnp.sum(dfiltered * extended[halo_rows - offset : halo_rows - offset + length], axis=0)
            for offset in range(halo_rows + 1)
        ],
        axis=0,
    )
    incoming = passed_along(dextended[:halo_rows], "ctx", -1)
    dlocal = dextended[halo_rows:] + jnp.concatenate(
        [jnp.zeros((length - halo_rows, 3, channels), jnp.float32), incoming], axis=0
    )
    feature_grad = dlocal.astype(jnp.bfloat16)[None]
    totals = lax.psum(
        (conv_local, rate_local, residue_local, skip_local, gain_local), ("dp", "ctx")
    )
    return (block_out[None], feature_grad, totals[0], totals[1], totals[2], totals[3], totals[4])


def solution(mesh):
    in_specs = (
        P("dp", "ctx", None, "mp"),
        P(None, None, "mp"),
        P(None, "mp"),
        P(None, "mp"),
        P("mp"),
        P("mp"),
        P("dp", "ctx", "mp"),
    )
    out_specs = (
        P("dp", "ctx", "mp"),
        P("dp", "ctx", None, "mp"),
        P(None, None, "mp"),
        P(None, "mp"),
        P(None, "mp"),
        P("mp"),
        P("mp"),
    )
    return jax.shard_map(local, mesh=mesh, in_specs=in_specs, out_specs=out_specs, check_vma=False)
```

profile of v0, /device:TPU:0, one launch (start us, length us, event | category | flops | bytes accessed | tf_op | source)
XLA Modules:
  0.0 2139.7 jit_solution(14530745588208930304)
XLA Ops:
  9.4 2.1 fusion.91
  12.5 7.9 fusion.48
  25.0 38.0 %while.51 = (s32[]{:T(128)}, f32[16,8,128,128]{3,2,1,0:T(8,128)}, f32[16,8]{1,0:T(8,128)S(1)}, f32[16,128,128]{2,1,0:T(8,128)}, s32[]{:T(128)}) while((s32[]{:T(128)}, f32[16,8,128,128]{3,2,1,0:T(8,128)}, f32[16,8]{1,0:T(8,128)S(1)}, f32[16,128,128]{2,1,0:T(8,128)}, s32[]{:T(128)}) %tuple.143), condition=%wide.region_1.2_spmd, body=%wide.region_0.1_spmd.sunk | while | flops 201654288 | bytes 754849 | solution.py:76
  25.1 2.3 fusion.110
  27.5 2.3 fusion.110
  29.9 2.3 fusion.110
  32.3 2.3 fusion.110
  34.6 2.3 fusion.110
  37.0 2.3 fusion.110
  39.4 2.3 fusion.110
  41.7 2.3 fusion.110
  44.1 2.3 fusion.110
  46.5 2.3 fusion.110
  48.9 2.3 fusion.110
  51.3 2.3 fusion.110
  53.6 2.3 fusion.110
  56.0 2.3 fusion.110
  58.3 2.3 fusion.110
  60.7 2.3 fusion.110
  63.0 9.9 copy.50
  76.2 91.5 %all-gather.3 = f32[64,16,8]{1,2,0:T(8,128)} all-gather(f32[1,16,8]{1,2,0:T(8,128)S(1)} %get-tuple-element.392), channel_id=2, replica_groups=mesh['dp'=4,'ctx'=64,'mp'=2] {'ctx'}, dimensions={0}, use_global_device_ids=true | all-gather | bytes 33280 | tf_op jit(solution)/shard_map/all_gather | solution.py:21
  169.1 53.8 %all-gather.7.cloned.1.call-done = f32[1024,8,1,128]{3,1,2,0:T(8,128)} async-done(((f32[16,8,1,128]{3,1,2,0:T(8,128)}), f32[1024,8,1,128]{3,1,2,0:T(8,128)}) %all-gather.7.cloned.1.call-update) | async-done | bytes 4194320 | tf_op jit(solution)/shard_map/all_gather | solution.py:21
  223.0 8.3 multiply_reduce_fusion.2
  232.6 2.5 all-reduce.5
  235.1 3.2 fusion.85
  239.3 1.6 fusion.87
  241.1 2.9 copy.51
  243.9 2.4 reshape.384
  246.3 2.4 reshape.382
  248.7 2.9 fusion.72
  252.8 232.8 %all-gather.9.cloned.1.call-done = f32[1024,8,128]{2,1,0:T(8,128)} async-done(((f32[16,8,128]{2,1,0:T(8,128)}), f32[1024,8,128]{2,1,0:T(8,128)}) %all-gather.9.cloned.1.call-update) | async-done | bytes 4194320 | tf_op jit(solution)/shard_map/all_gather | solution.py:21
  485.6 107.9 %while.53 = (s32[]{:T(128)}, f32[16,8,128]{2,1,0:T(8,128)S(1)}, s32[]{:T(128)}, f32[64,16,8]{1,2,0:T(8,128)}, f32[64,16,8,128]{3,2,1,0:T(8,128)}, /*index=5*/s32[]{:T(128)}, s32[]{:T(128)}, s32[]{:T(128)}, s32[]{:T(128)}) while((s32[]{:T(128)}, f32[16,8,128]{2,1,0:T(8,128)S(1)}, s32[]{:T(128)}, f32[64,16,8]{1,2,0:T(8,128)}, ...), condition=%wide.region_9.10_spmd, body=%wide.region_8.9_spmd.sunk | while | flops 32774 | bytes 199315 | solution.py:30
  594.1 146.1 %while.54 = (s32[]{:T(128)}, f32[16,8,128]{2,1,0:T(8,128)}, f32[16,8]{1,0:T(8,128)}, f32[16,128,128]{2,1,0:T(8,128)}, f32[16,128,128]{2,1,0:T(8,128)}, /*index=5...) while((s32[]{:T(128)}, f32[16,8,128]{2,1,0:T(8,128)}, ...), condition=%wide.region_15.16_spmd.clone, body=%wide.region_10.15_spmd.clone.sunk | while | flops 202687648 | bytes 3312593 | solution.py:144
  659.6 1.5 multiply_reduce_fusion.7
  668.7 1.5 multiply_reduce_fusion.7
  677.8 1.5 multiply_reduce_fusion.7
  686.9 1.5 multiply_reduce_fusion.7
  705.2 1.5 multiply_reduce_fusion.7
  714.3 1.5 multiply_reduce_fusion.7
  741.6 2.8 copy.59
  744.4 2.4 reshape.385
  746.8 2.9 slice_multiply_fusion.6
  751.2 3.4 fusion.54
  755.3 2.8 fusion.38
  758.1 1.7 copy-done.5
  762.0 1364.5 %all-reduce.3 = (f32[8,16]{1,0:T(8,128)}, f32[2048]{0:T(1024)}, f32[2048]{0:T(1024)}) all-reduce(f32[8,16]{1,0:T(8,128)S(1)} %bitcast_multiply_fusion.4, f32[2048]{0:T(1024)} %get-tuple-element.308, f32[2048]{0:T(1024)S(1)} %copy-done.24), channel_id=1, replica_groups=mesh['dp'=4,'ctx'=64,'mp'=2] {'dp','ctx'}, use_global_device_ids=true, to_apply=%region_24.25 | all-reduce | flops 4224 | bytes 33792 | tf_op jit(solution)/shard_map/psum | solution.py:171
  2126.5 3.5 fusion.57
  2130.0 1.7 copy.61
  (606 shorter events, 267.1 us)
Async XLA Ops:
  7.2 215.7 %all-gather.7.cloned.1.call-start = ((), (), s32[]{:S(2)}) async-start(), calls=%async_computation | async-start | bytes 4259840 | tf_op jit(solution)/shard_map/all_gather | solution.py:21
  8.1 4.3 collective-permute-start
  11.6 9.9 copy-start.12
  12.4 9.1 copy-start.14
  21.5 1.0 copy-start
  22.7 1.0 copy-start.6
  63.0 10.0 copy-start.26
  63.0 10.7 copy-start.23
  73.6 411.9 %all-gather.9.cloned.1.call-start = ((), (), s32[]{:S(2)}) async-start(), calls=%async_computation.1 | async-start | bytes 4259840 | tf_op jit(solution)/shard_map/all_gather | solution.py:21
  73.8 149.1 %copy-start.21 = (f32[16,8]{1,0:T(8,128)}, f32[16,8]{1,0:T(8,128)S(1)}, u32[]{:S(2)}) copy-start(f32[16,8]{1,0:T(8,128)S(1)} %copy.49) | copy-start | bytes 1540
  73.8 94.1 %copy-start.9 = (f32[16,8,16,128]{3,1,2,0:T(8,128)S(1)}, f32[16,8,16,128]{3,1,2,0:T(8,128)}, u32[]{:S(2)}) copy-start(f32[16,8,16,128]{3,1,2,0:T(8,128)} %get-tuple-element.382) | copy-start | bytes 3145732
  167.8 55.1 %copy-start.31 = (f32[128]{0:T(128)}, f32[128]{0:T(128)S(1)}, u32[]{:S(2)}) copy-start(f32[128]{0:T(128)S(1)} %iota_add_fusion) | copy-start | bytes 1540
  222.9 8.3 copy-start.1
  222.9 8.3 copy-start.7
  222.9 8.3 copy-start.16
  222.9 8.3 copy-start.18
  231.2 1.4 copy-start.3
  231.2 3.9 copy-start.19
  232.6 6.7 copy-start.22
  232.6 6.7 copy-start.32
  235.1 13.6 copy-start.29
  235.1 16.5 copy-start.27
  238.3 1.1 copy-start.8
  241.0 1888.9 %all-reduce.8.cloned.1.call-start = ((), (), s32[]{:S(2)}) async-start(), calls=%async_computation.2 | async-start | bytes 589824 | tf_op jit(solution)/shard_map/psum | solution.py:171
  248.7 2.9 copy-start.2
  248.7 2.9 copy-start.10
  740.2 6.6 copy-start.17
  740.2 6.6 copy-start.20
  740.2 6.6 copy-start.28
  740.2 6.6 copy-start.30
  749.8 1.4 copy-start.4
  754.6 0.8 copy-start.13
  754.6 0.8 copy-start.15
  755.3 6.6 copy-start.25
  755.3 6.7 copy-start.24
  758.1 1.7 copy-start.5
  759.8 1366.6 %collective-permute-start.1 = (f32[6,3,2048]{2,0,1:T(8,128)S(1)}, f32[6,3,2048]{2,0,1:T(8,128)S(1)}, u32[]{:S(2)}, u32[]{:S(2)}) collective-permute-start(f32[6,3,2048]{2,0,1:T(8,128)S(1)} %slice.156), channel_id=1, source_target_pairs={{2,0},{4,2},{6,4},{8,6},{10,8},{12,10},{14,12},{16,14},{18,16},{20... | collective-permute-start | bytes 442376 | tf_op jit(solution)/shard_map/ppermute | solution.py:14
  761.3 0.7 copy-start.11
Sparse Core Ops, SparseCore 0:
  73.8 149.0 all-gather.6
  241.1 244.3 all-gather.8
  762.1 380.4 all-reduce.7
where the time goes:
time: 2150 us; the launch traced here: 2140 us
  blocking collectives  1460 us (68%)
  waiting for transfers between devices  287 us (13%)
  local copies, waits for them, and re-layouts  156 us (7%)
  other arithmetic  156 us (7%)
  matrix products  62.4 us (3%)
    psum x1, blocking collectives, local(): lax.psum((conv_local, rate_local, residue_local, skip_local, gain_local),...  1360 us
    all_gather x2, waiting for transfers between devices, carried_in(): gathered = jax.tree.map(lambda a: lax.all_gather(a, axis), part)  287 us
    all_gather x1, blocking collectives, carried_in(): gathered = jax.tree.map(lambda a: lax.all_gather(a, axis), part)  91.5 us
    add x63, other arithmetic, compose_back(): return (earlier[0] * later[0], earlier[1] * later[0][..., None] + later[1])  58.2 us
    mul x126, local copies, waits for them, and re-layouts, compose_back(): return (earlier[0] * later[0], earlier[1] * later[0][..., None] + later[1])  47.7 us
  transfers between devices with their start and end apart: 5, of which 2 were waited for; matrix products, arithmetic and copies ran while one was open for 1% of the time, Pallas kernels for 0%

commit v1 on v0

--- a/solution.py
+++ b/solution.py
@@ -169,7 +169,7 @@
     )
     feature_grad = dlocal.astype(jnp.bfloat16)[None]
     totals = lax.psum(
-        (conv_local, rate_local, residue_local, skip_local, gain_local), ("dp", "ctx")
+        lax.psum((conv_local, rate_local, residue_local, skip_local, gain_local), "dp"), "ctx"
     )
     return (block_out[None], feature_grad, totals[0], totals[1], totals[2], totals[3], totals[4])
 

time: 2150 us -> 1310 us (0.61)
  blocking collectives: 1460 us -> 388 us
  waiting for transfers between devices: 287 us -> 532 us
    psum x1, blocking collectives: 1360 us -> 17 us  [local(): lax.psum((conv_local, rate_local, residue_local, skip_local, gain_local),...]
    psum x0 -> x1, blocking collectives: none -> 277 us  [local(): lax.psum(lax.psum((conv_local, rate_local, residue_local, skip_local, gai...]
    psum x0 -> x1, waiting for transfers between devices: none -> 247 us  [local(): lax.psum(lax.psum((conv_local, rate_local, residue_local, skip_local, gai...]
  transfers between devices with their start and end apart: 5 -> 6, of which waited for: 2 -> 3; matrix products, arithmetic and copies ran while one was open for 1% -> 2% of each run, Pallas kernels for 0% -> 0%
where the time goes in v1:
time: 1310 us; the launch traced here: 1290 us
  waiting for transfers between devices  532 us (41%)
  blocking collectives  388 us (30%)
  other arithmetic  154 us (12%)
  local copies, waits for them, and re-layouts  136 us (10%)
  matrix products  62.4 us (5%)
  between operations  14.1 us (1%)
    all_gather x2, waiting for transfers between devices, carried_in(): gathered = jax.tree.map(lambda a: lax.all_gather(a, axis), part)  286 us
    psum x1, blocking collectives, local(): lax.psum(lax.psum((conv_local, rate_local, residue_local, skip_local, gai...  277 us
    psum x1, waiting for transfers between devices, local(): lax.psum(lax.psum((conv_local, rate_local, residue_local, skip_local, gai...  247 us
    all_gather x1, blocking collectives, carried_in(): gathered = jax.tree.map(lambda a: lax.all_gather(a, axis), part)  92.1 us
    add x63, other arithmetic, compose_back(): return (earlier[0] * later[0], earlier[1] * later[0][..., None] + later[1])  58.2 us
    mul x126, local copies, waits for them, and re-layouts, compose_back(): return (earlier[0] * later[0], earlier[1] * later[0][..., None] + later[1])  47.7 us
    dot_general x16, matrix products, forward_plain(): return jnp.einsum('pts,sc->ptc', matrix, product_block, precision=HIGHEST)  36.8 us
    dynamic_update_slice x48, local copies, waits for them, and re-layouts, local(): lax.map(backward_adjoint, (rate_rows, grouped, dgrouped, states, weights,...  30.8 us
  transfers between devices with their start and end apart: 6, of which 3 were waited for; matrix products, arithmetic and copies ran while one was open for 2% of the time, Pallas kernels for 0%

profile of v1, /device:TPU:0, one launch (start us, length us, event | category | flops | bytes accessed | tf_op | source)
XLA Modules:
  0.0 1291.6 jit_solution(17466538137047817354)
XLA Ops:
  9.4 1.9 fusion.91
  12.3 7.5 fusion.48
  19.8 1.5 slice_bitcast_fusion
  25.1 38.0 %while.51 = (s32[]{:T(128)}, f32[16,8,128,128]{3,2,1,0:T(8,128)}, f32[16,8]{1,0:T(8,128)S(1)}, f32[16,128,128]{2,1,0:T(8,128)}, s32[]{:T(128)}) while((s32[]{:T(128)}, f32[16,8,128,128]{3,2,1,0:T(8,128)}, f32[16,8]{1,0:T(8,128)S(1)}, f32[16,128,128]{2,1,0:T(8,128)}, s32[]{:T(128)}) %tuple.146), condition=%wide.region_1.2_spmd, body=%wide.region_0.1_spmd.sunk | while | flops 201654288 | bytes 754849 | solution.py:76
  25.2 2.3 fusion.110
  27.6 2.4 fusion.110
  30.1 2.3 fusion.110
  32.4 2.3 fusion.110
  34.8 2.3 fusion.110
  37.2 2.3 fusion.110
  39.5 2.3 fusion.110
  41.9 2.3 fusion.110
  44.3 2.3 fusion.110
  46.7 2.3 fusion.110
  49.1 2.3 fusion.110
  51.4 2.3 fusion.110
  53.8 2.3 fusion.110
  56.1 2.3 fusion.110
  58.5 2.3 fusion.110
  60.9 2.3 fusion.110
  63.2 9.9 copy.50
  76.4 92.1 %all-gather.3 = f32[64,16,8]{1,2,0:T(8,128)} all-gather(f32[1,16,8]{1,2,0:T(8,128)S(1)} %get-tuple-element.397), channel_id=2, replica_groups=mesh['dp'=4,'ctx'=64,'mp'=2] {'ctx'}, dimensions={0}, use_global_device_ids=true | all-gather | bytes 33280 | tf_op jit(solution)/shard_map/all_gather | solution.py:21
  169.7 53.5 %all-gather.7.cloned.1.call-done = f32[1024,8,1,128]{3,1,2,0:T(8,128)} async-done(((f32[16,8,1,128]{3,1,2,0:T(8,128)}), f32[1024,8,1,128]{3,1,2,0:T(8,128)}) %all-gather.7.cloned.1.call-update) | async-done | bytes 4194320 | tf_op jit(solution)/shard_map/all_gather | solution.py:21
  223.3 9.2 multiply_reduce_fusion.2
  232.5 2.9 fusion.67
  235.4 2.4 all-reduce.7
  237.8 3.2 fusion.85
  242.1 1.6 fusion.87
  243.8 2.9 copy.51
  246.7 2.4 reshape.384
  249.0 2.4 reshape.382
  251.4 2.8 fusion.72
  254.2 2.4 fusion.81
  256.6 232.0 %all-gather.9.cloned.1.call-done = f32[1024,8,128]{2,1,0:T(8,128)} async-done(((f32[16,8,128]{2,1,0:T(8,128)}), f32[1024,8,128]{2,1,0:T(8,128)}) %all-gather.9.cloned.1.call-update) | async-done | bytes 4194320 | tf_op jit(solution)/shard_map/all_gather | solution.py:21
  488.6 107.7 %while.53 = (s32[]{:T(128)}, f32[16,8,128]{2,1,0:T(8,128)S(1)}, s32[]{:T(128)}, f32[64,16,8]{1,2,0:T(8,128)}, f32[64,16,8,128]{3,2,1,0:T(8,128)}, /*index=5*/s32[]{:T(128)}, s32[]{:T(128)}, s32[]{:T(128)}, s32[]{:T(128)}) while((s32[]{:T(128)}, f32[16,8,128]{2,1,0:T(8,128)S(1)}, s32[]{:T(128)}, f32[64,16,8]{1,2,0:T(8,128)}, ...), condition=%wide.region_9.10_spmd, body=%wide.region_8.9_spmd.sunk | while | flops 32774 | bytes 199315 | solution.py:30
  596.3 114.5 %while.54 = (s32[]{:T(128)}, f32[16,8,128]{2,1,0:T(8,128)S(1)}, f32[16,8]{1,0:T(8,128)}, f32[16,128,128]{2,1,0:T(8,128)}, f32[16,128,128]{2,1,0:T(8,128)}, /*ind...) while((s32[]{:T(128)}, f32[16,8,128]{2,1,0:T(8,128)S(1)}, ...), condition=%wide.region_15.16_spmd.clone, body=%wide.region_10.15_spmd.clone.sunk | while | flops 202687648 | bytes 3312085 | solution.py:144
  618.7 1.5 multiply_reduce_fusion.7
  710.8 2.8 copy.59
  713.7 2.4 reshape.385
  716.0 2.7 slice_multiply_fusion.6
  718.8 2.0 pad_maximum_fusion.1
  720.9 3.4 fusion.54
  729.4 5.9 fusion.38
  738.3 17.0 %all-reduce.5 = (f32[8,16]{1,0:T(8,128)S(1)}, f32[2048]{0:T(1024)S(1)}, f32[2048]{0:T(1024)S(1)}) all-reduce(f32[8,16]{1,0:T(8,128)S(1)} %bitcast_multiply_fusion.4, f32[2048]{0:T(1024)} %get-tuple-element.308, f32[2048]{0:T(1024)S(1)} %get-tuple-element.307), channel_id=1, replica_groups=mesh['dp'=4,'ctx'=64,'mp'=2] {'dp'}, use_global_device_ids=true, to_apply=%region_25.26 | all-reduce | flops 4224 | bytes 33792 | tf_op jit(solution)/shard_map/psum | solution.py:172
  755.3 276.6 %all-reduce.3 = (f32[8,16]{1,0:T(8,128)}, f32[2048]{0:T(1024)}, f32[2048]{0:T(1024)}) all-reduce(f32[8,16]{1,0:T(8,128)S(1)} %get-tuple-element.364, f32[2048]{0:T(1024)S(1)} %get-tuple-element.365, f32[2048]{0:T(1024)S(1)} %get-tuple-element.366), channel_id=1, replica_groups=mesh['dp'=4,'ctx'=64,'mp'=2] {'ctx'}, use_global_device_ids=true, to_apply=%region_26.27 | all-reduce | flops 4224 | bytes 33792 | tf_op jit(solution)/shard_map/psum | solution.py:171
  1031.9 3.5 fusion.57
  1035.4 246.5 %all-reduce.11.cloned.1.call-done = (f32[7,3,2048]{2,1,0:T(4,128)}, f32[8,2048]{1,0:T(8,128)}) async-done(((f32[7,3,2048]{2,1,0:T(4,128)}, f32[8,2048]{1,0:T(8,128)}), (f32[7,3,2048]{2,1,0:T(4,128)}, f32[8,2048]{1,0:T(8,128)})) %all-reduce.11.cloned.1.call-update) | async-done | bytes 237584 | tf_op jit(solution)/shard_map/psum | solution.py:171
  1281.9 1.7 copy.61
  (586 shorter events, 241.5 us)
Async XLA Ops:
  7.2 216.1 %all-gather.7.cloned.1.call-start = ((), (), s32[]{:S(2)}) async-start(), calls=%async_computation | async-start | bytes 4259840 | tf_op jit(solution)/shard_map/all_gather | solution.py:21
  8.1 4.2 collective-permute-start
  11.3 10.0 copy-start.6
  11.3 10.0 copy-start.7
  11.4 9.9 copy-start.8
  11.4 9.9 copy-start.9
  11.4 9.9 copy-start.10
  11.5 9.9 copy-start.11
  12.2 9.2 copy-start.12
  22.8 1.0 copy-start.1
  63.2 10.0 copy-start.18
  63.2 10.7 copy-start.17
  73.8 414.8 %all-gather.9.cloned.1.call-start = ((), (), s32[]{:S(2)}) async-start(), calls=%async_computation.1 | async-start | bytes 4259840 | tf_op jit(solution)/shard_map/all_gather | solution.py:21
  73.9 94.6 %copy-start.4 = (f32[16,8,16,128]{3,1,2,0:T(8,128)S(1)}, f32[16,8,16,128]{3,1,2,0:T(8,128)}, u32[]{:S(2)}) copy-start(f32[16,8,16,128]{3,1,2,0:T(8,128)} %get-tuple-element.387) | copy-start | bytes 3145732
  75.2 148.1 %copy-start.15 = (f32[8,2048]{1,0:T(8,128)S(1)}, f32[8,2048]{1,0:T(8,128)}, u32[]{:S(2)}) copy-start(f32[8,2048]{1,0:T(8,128)} %param.18) | copy-start | bytes 196612
  223.3 9.2 copy-start.2
  223.3 9.2 copy-start.14
  223.3 9.2 copy-start.16
  237.8 13.6 %copy-start.19 = (f32[128]{0:T(128)}, f32[128]{0:T(128)S(1)}, u32[]{:S(2)}) copy-start(f32[128]{0:T(128)S(1)} %get-tuple-element.398) | copy-start | bytes 1540
  241.0 1.1 copy-start.3
  243.7 788.1 %all-reduce.13.cloned.1.call-start = ((), (), s32[]{:S(2)}) async-start(), calls=%async_computation.3 | async-start | bytes 589824 | tf_op jit(solution)/shard_map/psum | solution.py:172
  251.4 2.9 copy-start.5
  710.8 7.9 copy-start.13
  710.8 5.2 copy-start.20
  718.8 2.0 copy-start
  729.1 552.8 %all-reduce.11.cloned.1.call-start = ((), (), s32[]{:S(2)}) async-start(), calls=%async_computation.2 | async-start | bytes 589824 | tf_op jit(solution)/shard_map/psum | solution.py:171
  737.0 294.9 %collective-permute-start.1 = (f32[6,3,2048]{2,0,1:T(8,128)S(1)}, f32[6,3,2048]{2,0,1:T(8,128)S(1)}, u32[]{:S(2)}, u32[]{:S(2)}) collective-permute-start(f32[6,3,2048]{2,0,1:T(8,128)S(1)} %slice.156), channel_id=1, source_target_pairs={{2,0},{4,2},{6,4},{8,6},{10,8},{12,10},{14,12},{16,14},{18,16},{20... | collective-permute-start | bytes 442376 | tf_op jit(solution)/shard_map/ppermute | solution.py:14
Sparse Core Ops, SparseCore 0:
  73.9 149.2 all-gather.6
  243.9 244.6 all-gather.8
  729.2 45.9 all-reduce.12
  1032.0 249.8 all-reduce.10
